TPU v7x, 32 devices: a whole 2x2x4 slice. The times are simulated.
32 devices in a mesh: box: 8 (over y, x, core), dir: 4 (over z).
Axes of the slice: x: 2, y: 2, z: 4, core: 2. Of those that a mesh axis runs over, the one named last changes fastest.
Arguments:
- fine_out: float32 [1024, 2, 8192], P(('box', 'dir')), may hold values from -6 to 6
- theta_interp: float32 [128, 64], replicated, may hold values from -0.75 to 0.75
- phi_interp: float32 [128, 256], replicated, may hold values from -0.5 to 0.5
- shift_phase: float32 [8, 32768], P(None, 'dir'), may hold values from -3.140625 to 3.140625
- translation: float32 [316, 2, 32768], P(None, None, 'dir'), may hold values from -0.25 to 0.25
- upper_in: float32 [128, 2, 32768], P('box', None, 'dir'), may hold values from -6 to 6
- children: int32 [128, 8], P('box'), may hold values from 0 to 1023, as said below
- far_boxes: int32 [128, 28], P('box'), may hold values from 0 to 127, as said below
- far_offsets: int32 [128, 28], P('box'), may hold values from 0 to 315
Outputs:
- coarse_in: float32 [128, 2, 32768], P('box', None, 'dir')
- fine_in: float32 [1024, 2, 8192], P(('box', 'dir'))
Inputs may be any that keep to these rules, and one draw needn't show every extreme that they name: Every fine box is named exactly once. The coarse boxes i * 16 to (i + 1) * 16 - 1 have as children exactly the fine boxes 8 * i * 16 to 8 * (i + 1) * 16 - 1. `far_boxes`: each row names 28 different coarse boxes, never the row's own box.
All inputs are finite; a program needn't handle non-finite values.
Results may differ from a plain program's by a relative error of at most 0.00008.
Values sent between devices are 32-bit elements; how exact they have to be, the bound alone decides.
A program may use at most 192 MiB of HBM per device.

v0:
```python
import jax
import jax.numpy as jnp
from jax import lax
from jax.sharding import PartitionSpec as P

HIGHEST_PREC = lax.Precision.HIGHEST


def interpolate(patterns, theta_map, phi_map):
    amount = patterns.shape[0]
    coarse_theta, fine_theta = theta_map.shape
    fine_phi, coarse_phi = phi_map.shape
    flat_rows = patterns.reshape(amount * 2 * fine_theta, fine_phi)
    along_phi = jnp.dot(
        flat_rows, phi_map, precision=HIGHEST_PREC, preferred_element_type=jnp.float32
    )
    along_phi = along_phi.reshape(amount * 2, fine_theta, coarse_phi)
    result = jnp.einsum("tu,nus->nts", theta_map, along_phi, precision=HIGHEST_PREC)
    return result.reshape(amount, 2, coarse_theta * coarse_phi)


def anterpolate(patterns, theta_map, phi_map):
    amount = patterns.shape[0]
    coarse_theta, fine_theta = theta_map.shape
    fine_phi, coarse_phi = phi_map.shape
    flat_rows = patterns.reshape(amount * 2 * coarse_theta, coarse_phi)
    along_phi = lax.dot_general(
        flat_rows,
        phi_map,
        (((1,), (1,)), ((), ())),
        precision=HIGHEST_PREC,
        preferred_element_type=jnp.float32,
    )
    along_phi = along_phi.reshape(amount * 2, coarse_theta, fine_phi)
    result = jnp.einsum("tu,nts->nus", theta_map, along_phi, precision=HIGHEST_PREC)
    return result.reshape(amount, 2, fine_theta * fine_phi)


def aggregate(child_rows, child_index, cosine, sine):
    picked = child_rows[child_index]
    real_part = jnp.sum(cosine * picked[:, :, 0] - sine * picked[:, :, 1], axis=1)
    imag_part = jnp.sum(sine * picked[:, :, 0] + cosine * picked[:, :, 1], axis=1)
    return jnp.stack([real_part, imag_part], axis=1)


def translate(sources, far_index, far_kind, operators):
    source_rows = sources[far_index]
    kernel_rows = operators[far_kind]
    real_part = jnp.sum(
        kernel_rows[:, :, 0] * source_rows[:, :, 0] - kernel_rows[:, :, 1] * source_rows[:, :, 1],
        axis=1,
    )
    imag_part = jnp.sum(
        kernel_rows[:, :, 0] * source_rows[:, :, 1] + kernel_rows[:, :, 1] * source_rows[:, :, 0],
        axis=1,
    )
    return jnp.stack([real_part, imag_part], axis=1)


def disaggregate(incoming, child_index, cosine, sine, total):
    flat_index = child_index.reshape(-1)
    slot_count = flat_index.shape[0]
    owner = (
        jnp.zeros((total,), jnp.int32).at[flat_index].set(jnp.arange(slot_count, dtype=jnp.int32))
    )
    parent = owner // 8
    octant = owner % 8
    parent_rows = incoming[parent]
    cos_rows = cosine[octant]
    sin_rows = sine[octant]
    real_in = parent_rows[:, 0]
    imag_in = parent_rows[:, 1]
    real_part = cos_rows * real_in + sin_rows * imag_in
    imag_part = cos_rows * imag_in - sin_rows * real_in
    return jnp.stack([real_part, imag_part], axis=1)


def shards(
    fine_out,
    theta_interp,
    phi_interp,
    shift_phase,
    translation,
    upper_in,
    children,
    far_boxes,
    far_offsets,
):
    child_rows = interpolate(fine_out, theta_interp, phi_interp)
    gathered = lax.all_to_all(child_rows, "dir", split_axis=2, concat_axis=0, tiled=True)
    span_rows = gathered.shape[0]
    local_index = children % span_rows
    cosine = jnp.cos(shift_phase)
    sine = jnp.sin(shift_phase)
    outgoing = aggregate(gathered, local_index, cosine, sine)
    every_box = lax.all_gather(outgoing, "box", axis=0, tiled=True)
    coarse_in = translate(every_box, far_boxes, far_offsets, translation) + upper_in
    child_in = disaggregate(coarse_in, local_index, cosine, sine, span_rows)
    returned = lax.all_to_all(child_in, "dir", split_axis=0, concat_axis=2, tiled=True)
    fine_in = anterpolate(returned, theta_interp, phi_interp)
    return (coarse_in, fine_in)


def solution(mesh):
    placed = (
        P(("box", "dir"), None, None),
        P(),
        P(),
        P(None, "dir"),
        P(None, None, "dir"),
        P("box", None, "dir"),
        P("box", None),
        P("box", None),
        P("box", None),
    )
    return jax.shard_map(
        shards,
        mesh=mesh,
        in_specs=placed,
        out_specs=(P("box", None, "dir"), P(("box", "dir"), None, None)),
        check_vma=False,
    )
```

profile of v0, /device:TPU:0, one launch (start us, length us, event | category | flops | bytes accessed | tf_op | source)
XLA Modules:
  0.0 969.6 jit_solution(1580979285283009620)
XLA Ops:
  7.2 3.1 dot_general.16
  10.3 3.5 fusion.8
  13.8 15.6 %convolution_bitcast_fusion = f32[64,128,256]{1,2,0:T(8,128)} fusion(f32[64,64,256]{2,1,0:T(8,128)S(1)} %fusion.8, f32[128,64]{0,1:T(8,128)S(1)} %copy-done.4), kind=kOutput, calls=%fused_computation.24 | convolution fusion | flops 1610612736 | bytes 12615680 | tf_op jit(solution)/shard_map/tu,nus->nts/dot_general | solution.py:18
  29.4 9.0 copy.50
  38.4 11.1 %reshape.62 = f32[32,2,32768]{2,1,0:T(2,128)} reshape(f32[64,128,256]{2,1,0:T(8,128)} %copy.50) | data formatting | bytes 16777216 | tf_op jit(solution)/shard_map/reshape | solution.py:19
  49.5 43.1 %copy.51 = f32[32,2,32768]{0,1,2:T(2,128)} copy(f32[32,2,32768]{2,1,0:T(2,128)} %reshape.62) | data formatting | bytes 16777216 | tf_op jit(solution)/shard_map/reshape | solution.py:19
  92.7 38.6 %reshape.134 = f32[4,1,524288]{2,1,0:T(1,128)} reshape(f32[32768,2,32]{2,1,0:T(2,128)} %bitcast.65) | data formatting | bytes 16777216
  131.3 6.5 all-to-all-start
  138.9 182.9 %all-to-all-done = f32[4,1,524288]{2,1,0:T(1,128)} async-done(((f32[4,1,524288]{2,1,0:T(1,128)}), f32[4,1,524288]{2,1,0:T(1,128)}, u32[]{:S(2)}, u32[]{:S(2)}) %all-to-all-start) | async-done | bytes 8388640 | tf_op jit(solution)/shard_map/all_to_all | solution.py:90
  322.3 28.4 %reduce.2 = f32[4,524288]{1,0:T(4,128)} reduce(f32[4,1,524288]{2,1,0:T(1,128)} %all-to-all-done, f32[]{:T(128)} %broadcast.87), dimensions={1}, to_apply=%all_to_all.24.reduce_sub_computation | reduce | bytes 16777220 | tf_op jit(solution)/shard_map/all_to_all | solution.py:90
  350.7 62.9 %reshape.135 = f32[32768,2,32]{2,1,0:T(2,128)} reshape(f32[4,524288]{1,0:T(4,128)} %reduce.2) | data formatting | bytes 16777216
  413.6 43.4 %copy.64 = f32[32,2,4,8192]{3,2,0,1:T(4,128)} copy(f32[32,2,4,8192]{0,1,3,2:T(2,128)} %bitcast.66) | data formatting | bytes 16777216 | tf_op jit(solution)/shard_map/all_to_all | solution.py:90
  457.0 8.2 copy.53
  465.3 8.1 copy.55
  473.4 15.8 %gather_fusion.1 = f32[128,2,8192]{2,1,0:T(2,128)} fusion(f32[128,2,8192]{2,1,0:T(2,128)} %copy.55, s32[1024]{0:T(1024)S(1)} %pad_clamp_fusion.3), kind=kCustom, calls=%fused_computation.1 | custom fusion | bytes 16777728 | tf_op jit(solution)/shard_map/gather | solution.py:40
  489.2 11.5 %fusion.17 = (f32[16,8,1,8192]{3,2,1,0:T(1,128)S(1)}, f32[16,8,1,8192]{3,2,1,0:T(1,128)S(1)}) fusion(f32[16,8,2,8192]{3,2,1,0:T(2,128)} %bitcast.70), kind=kLoop, calls=%fused_computation.58 | loop fusion | bytes 16777216 | tf_op jit(solution)/shard_map/slice | solution.py:41
  500.8 10.4 %fusion.1 = (f32[16,8192]{1,0:T(8,128)S(1)}, f32[16,8192]{1,0:T(8,128)S(1)}) fusion(f32[16,8,1,8192]{3,2,1,0:T(1,128)S(1)} %get-tuple-element.11, f32[16,8,1,8192]{3,2,1,0:T(1,128)S(1)} %get-tuple-element.10, f32[8,8192]{1,0:T(8,128)S(1)} %get-tuple-element.13, f32[8,8192]{1,0:T(8,128)S(1)} %get-tuple-element.12), kind=kLoop, calls=%fused_computation.15 | loop fusion | flops 8126464 | bytes 9961472 | tf_op jit(solution)/shard_map/reduce_sum | solution.py:41
  515.6 3.7 gather_fusion.3
  519.3 3.7 gather_fusion.5
  523.3 45.4 %gather_fusion = f32[448,2,8192]{2,1,0:T(2,128)} fusion(f32[316,2,8192]{2,1,0:T(2,128)} %param.13, s32[1024]{0:T(1024)S(1)} %pad_clamp_fusion.4), kind=kCustom, calls=%fused_computation | custom fusion | bytes 58722048 | tf_op jit(solution)/shard_map/gather | solution.py:48
  568.7 41.9 %gather_fusion.2 = f32[448,2,8192]{2,1,0:T(2,128)} fusion(f32[128,2,8192]{2,1,0:T(2,128)} %all-gather.2.cloned.1.call-done, s32[1024]{0:T(1024)S(1)} %pad_clamp_fusion.2), kind=kCustom, calls=%fused_computation.2 | custom fusion | bytes 58722048 | tf_op jit(solution)/shard_map/gather | solution.py:47
  610.5 72.5 %subtract_reduce_fusion = (f32[16,8192]{1,0:T(8,128)S(1)}, f32[16,8192]{1,0:T(8,128)S(1)}) fusion(f32[16,28,2,8192]{3,2,1,0:T(2,128)} %bitcast.68, f32[16,28,2,8192]{3,2,1,0:T(2,128)} %bitcast.67), kind=kLoop, calls=%fused_computation.8 | loop fusion | flops 29097984 | bytes 59768832 | tf_op jit(solution)/shard_map/reduce_sum | solution.py:49
  685.3 12.9 %gather_fusion.4 = f32[128,2,8192]{2,1,0:T(2,128)} fusion(f32[16,2,8192]{2,1,0:T(2,128)S(1)} %maximum_add_fusion, s32[1024]{0:T(1024)S(1)} %get-tuple-element.18), kind=kCustom, calls=%fused_computation.4 | custom fusion | bytes 16777728 | tf_op jit(solution)/shard_map/gather | solution.py:68
  698.1 11.8 %fusion.16 = (f32[128,1,8192]{2,1,0:T(1,128)}, f32[128,1,8192]{2,1,0:T(1,128)}) fusion(f32[128,2,8192]{2,1,0:T(2,128)} %gather_fusion.4), kind=kLoop, calls=%fused_computation.57 | loop fusion | bytes 16777216 | tf_op jit(solution)/shard_map/slice | solution.py:71
  710.0 16.0 %fusion.4 = (f32[128,1,8192]{2,0,1:T(8,128)S(1)}, f32[128,1,8192]{2,0,1:T(8,128)}) fusion(f32[128,8192]{1,0:T(8,128)} %gather_fusion.5, f32[128,8192]{1,0:T(8,128)} %gather_fusion.3, f32[128,1,8192]{2,1,0:T(1,128)} %get-tuple-element.9, f32[128,1,8192]{2,1,0:T(1,128)} %get-tuple-element.8), kind=kLoop, calls=%fused_computation.20 | loop fusion | flops 6291456 | bytes 25165824 | tf_op jit(solution)/shard_map/add | solution.py:73
  726.0 2.8 pad_maximum_fusion
  728.7 7.5 copy.62
  736.3 187.6 %all_to_all.33 = f32[128,2,8192]{2,1,0:T(2,128)} all-to-all(f32[128,2,8192]{2,1,0:T(2,128)S(1)} %copy.62), channel_id=1, replica_groups=mesh['box'=8,'dir'=4] {'dir'}, dimensions={0} | all-to-all | bytes 16777216 | tf_op jit(solution)/shard_map/all_to_all | solution.py:99
  923.8 13.8 %copy.81 = f32[4,32,2,8192]{3,0,2,1:T(4,128)} copy(f32[4,32,2,8192]{3,2,1,0:T(2,128)} %bitcast.72) | data formatting | bytes 16777216 | tf_op jit(solution)/shard_map/all_to_all | solution.py:99
  937.6 10.9 %dot_general.19 = f32[64,128,256]{2,1,0:T(8,128)} reshape(f32[32,2,4,8192]{3,2,1,0:T(4,128)} %bitcast.73) | data formatting | bytes 16777216 | tf_op jit(solution)/shard_map/dot_general | solution.py:27
  948.5 9.3 fusion.6
  957.8 2.5 convolution_bitcast_fusion.1
  (47 shorter events, 10.7 us)
Async XLA Ops:
  7.2 3.1 copy-start
  10.3 3.5 copy-start.4
  131.3 6.5 copy-start.8
  131.3 6.7 copy-start.3
  131.3 190.5 %all-to-all-start = ((f32[4,1,524288]{2,1,0:T(1,128)}), f32[4,1,524288]{2,1,0:T(1,128)}, u32[]{:S(2)}, u32[]{:S(2)}) async-start(f32[4,1,524288]{2,1,0:T(1,128)} %reshape.134), calls=%async_computation | async-start | bytes 16777216 | tf_op jit(solution)/shard_map/all_to_all | solution.py:90
  137.8 430.9 %all-gather.2.cloned.1.call-start = ((), (), s32[]{:S(2)}) async-start(), calls=%async_computation.2 | async-start | bytes 9437184 | tf_op jit(solution)/shard_map/all_gather | solution.py:96
  519.3 3.7 copy-start.6
  519.3 3.8 copy-start.7
  610.5 73.6 %copy-start.2 = (f32[16,2,8192]{2,1,0:T(2,128)S(1)}, f32[16,2,8192]{2,1,0:T(2,128)}, u32[]{:S(2)}) copy-start(f32[16,2,8192]{2,1,0:T(2,128)} %param.14) | copy-start | bytes 3145732
  685.3 12.9 %copy-start.1 = (f32[16,2,8192]{2,1,0:T(2,128)}, f32[16,2,8192]{2,1,0:T(2,128)S(1)}, u32[]{:S(2)}) copy-start(f32[16,2,8192]{2,1,0:T(2,128)S(1)} %maximum_add_fusion) | copy-start | bytes 3145732
  948.5 9.3 copy-start.5
Sparse Core Ops, SparseCore 0:
  514.5 53.5 all-gather.1
where the time goes:
time: 981 us; the launch traced here: 970 us
  local copies, waits for them, and re-layouts  414 us (42%)
  blocking collectives  188 us (19%)
  waiting for transfers between devices  183 us (19%)
  other arithmetic  133 us (14%)
  matrix products  30.9 us (3%)
  between operations  14.5 us (1%)
    all_to_all x1, blocking collectives, shards(): lax.all_to_all(child_in, 'dir', split_axis=0, concat_axis=2, tiled=True)  188 us
    all_to_all x1, waiting for transfers between devices, shards(): lax.all_to_all(child_rows, 'dir', split_axis=2, concat_axis=0, tiled=True)  183 us
    unnamed x20, local copies, waits for them, and re-layouts  102 us
    reduce_sum x1, other arithmetic, translate(): jnp.sum(kernel_rows[:, :, 0] * source_rows[:, :, 0] - kernel_rows[:, :, 1...  72.5 us
    all_to_all x4, local copies, waits for them, and re-layouts, shards(): lax.all_to_all(child_rows, 'dir', split_axis=2, concat_axis=0, tiled=True)  60.3 us
    reshape x2, local copies, waits for them, and re-layouts, interpolate(): return result.reshape(amount, 2, coarse_theta * coarse_phi)  54.2 us
    gather x1, local copies, waits for them, and re-layouts, translate(): kernel_rows = operators[far_kind]  45.4 us
    gather x1, local copies, waits for them, and re-layouts, translate(): source_rows = sources[far_index]  41.9 us
  transfers between devices with their start and end apart: 2, of which 1 were waited for; matrix products, arithmetic and copies ran while one was open for 6% of the time, Pallas kernels for 0%

commit v1 on v0

v1 whole, which is shorter than its diff:
```python
import functools

import jax
import jax.numpy as jnp
from jax import lax
from jax.experimental import pallas as pl
from jax.experimental.pallas import tpu as pltpu
from jax.sharding import PartitionSpec as P

F32, BF16 = jnp.float32, jnp.bfloat16
VMEM_BYTES = 52 * 1024 * 1024


def split(x):
    hi = x.astype(BF16)
    return hi, (x - hi.astype(F32)).astype(BF16)


def dot3(a, b):
    (ah, al), (bh, bl) = a, b
    d = functools.partial(jnp.dot, preferred_element_type=F32)
    return d(ah, bh) + (d(ah, bl) + d(al, bh))


def rows_view(x):
    n, _, k = x.shape
    return x.reshape(n, 2, k // 128, 128).transpose(0, 2, 1, 3).reshape(n, k // 64, 128)


def rows_unview(x):
    n, r, _ = x.shape
    return x.reshape(n, r // 2, 2, 128).transpose(0, 2, 1, 3).reshape(n, 2, r * 64)


def gather_up_kernel(group, parent, octant, x_ref, theta_ref, phi_ref, cs_ref, out_ref):
    step = pl.program_id(0)
    nd, tl = out_ref.shape[0], out_ref.shape[3]
    tc = nd * tl

    @pl.when(step == 0)
    def _():
        out_ref[...] = jnp.zeros_like(out_ref)

    theta = split(theta_ref[...])
    phi = split(phi_ref[...])
    rows = x_ref.shape[1]
    along = dot3(split(x_ref[...].reshape(group * rows, x_ref.shape[2])), phi)
    for g in range(group):
        p, o = parent[step * group + g], octant[step * group + g]
        full = dot3(theta, split(along[g * rows : (g + 1) * rows]))
        for j in range(nd):
            re = full[j * tl : (j + 1) * tl]
            im = full[tc + j * tl : tc + (j + 1) * tl]
            c, s = cs_ref[j, 0, o], cs_ref[j, 1, o]
            out_ref[j, p, 0] += c * re - s * im
            out_ref[j, p, 1] += s * re + c * im


def gather_up(x, theta2, phi, cs, parent, octant, parents):
    n, rows, lanes = x.shape
    nd, _, _, tl, pc = cs.shape
    group = 4
    return pl.pallas_call(
        functools.partial(gather_up_kernel, group),
        grid_spec=pltpu.PrefetchScalarGridSpec(
            num_scalar_prefetch=2,
            grid=(n // group,),
            in_specs=[
                pl.BlockSpec((group, rows, lanes), lambda i, *_: (i, 0, 0)),
                pl.BlockSpec(theta2.shape, lambda i, *_: (0, 0)),
                pl.BlockSpec(phi.shape, lambda i, *_: (0, 0)),
                pl.BlockSpec(cs.shape, lambda i, *_: (0, 0, 0, 0, 0)),
            ],
            out_specs=pl.BlockSpec((nd, parents, 2, tl, pc), lambda i, *_: (0, 0, 0, 0, 0)),
        ),
        out_shape=jax.ShapeDtypeStruct((nd, parents, 2, tl, pc), F32),
        compiler_params=pltpu.CompilerParams(vmem_limit_bytes=VMEM_BYTES),
    )(parent, octant, x, theta2, phi, cs)


def translate_kernel(far, kind, q_ref, trans_ref, upper_ref, rows_ref, plane_ref, buf, sem):
    p = pl.program_id(0)
    count, many = pl.num_programs(0), far.shape[1]
    tl = q_ref.shape[2]

    def start(row, slot):
        for l in range(many):
            pltpu.make_async_copy(trans_ref.at[kind[row, l]], buf.at[slot, l], sem.at[slot]).start()

    @pl.when(p == 0)
    def _():
        start(0, 0)

    @pl.when(p + 1 < count)
    def _():
        start(p + 1, (p + 1) % 2)

    slot = p % 2
    pltpu.make_async_copy(trans_ref.at[pl.ds(0, many)], buf.at[slot], sem.at[slot]).wait()
    for t in range(0, tl, 8):
        for h in range(2):
            re = im = None
            for l in range(many):
                f = far[p, l]
                q0 = q_ref[f, 0, t : t + 8, h * 128 : (h + 1) * 128]
                q1 = q_ref[f, 1, t : t + 8, h * 128 : (h + 1) * 128]
                a0 = buf[slot, l, pl.ds(t * 4 + h * 2, 8, stride=4), :]
                a1 = buf[slot, l, pl.ds(t * 4 + h * 2 + 1, 8, stride=4), :]
                r, i = a0 * q0 - a1 * q1, a0 * q1 + a1 * q0
                re = r if re is None else re + r
                im = i if im is None else im + i
            for c, total in ((0, re), (1, im)):
                where = pl.ds(t * 4 + h * 2 + c, 8, stride=4)
                total = total + upper_ref[0, where, :]
                rows_ref[0, where, :] = total
                plane_ref[0, c, t : t + 8, h * 128 : (h + 1) * 128] = total


def translate(q, trans, upper, far, kind):
    parents, rows, lanes = upper.shape
    _, _, tl, pc = q.shape
    many = far.shape[1]
    return pl.pallas_call(
        translate_kernel,
        grid_spec=pltpu.PrefetchScalarGridSpec(
            num_scalar_prefetch=2,
            grid=(parents,),
            in_specs=[
                pl.BlockSpec(q.shape, lambda i, *_: (0, 0, 0, 0)),
                pl.BlockSpec(memory_space=pl.ANY),
                pl.BlockSpec((1, rows, lanes), lambda i, *_: (i, 0, 0)),
            ],
            out_specs=[
                pl.BlockSpec((1, rows, lanes), lambda i, *_: (i, 0, 0)),
                pl.BlockSpec((1, 2, tl, pc), lambda i, *_: (i, 0, 0, 0)),
            ],
            scratch_shapes=[
                pltpu.VMEM((2, many, rows, lanes), F32),
                pltpu.SemaphoreType.DMA((2,)),
            ],
        ),
        out_shape=[
            jax.ShapeDtypeStruct((parents, rows, lanes), F32),
            jax.ShapeDtypeStruct((parents, 2, tl, pc), F32),
        ],
        compiler_params=pltpu.CompilerParams(vmem_limit_bytes=VMEM_BYTES),
    )(far, kind, q, trans, upper)


def spread_down_kernel(group, parent, octant, in_ref, theta_ref, phi_ref, cs_ref, out_ref, full):
    step = pl.program_id(0)
    nd, tl = in_ref.shape[0], in_ref.shape[3]
    tc = nd * tl
    theta = split(theta_ref[...])
    phi = split(phi_ref[...])
    parts = []
    for g in range(group):
        p, o = parent[step * group + g], octant[step * group + g]
        for j in range(nd):
            re, im = in_ref[j, p, 0], in_ref[j, p, 1]
            c, s = cs_ref[j, 0, o], cs_ref[j, 1, o]
            full[g, j * tl : (j + 1) * tl] = c * re + s * im
            full[g, tc + j * tl : tc + (j + 1) * tl] = c * im - s * re
        parts.append(dot3(theta, split(full[g])))
    along = jnp.concatenate(parts, axis=0)
    out_ref[...] = dot3(split(along), phi).reshape(out_ref.shape)


def spread_down(incoming, theta2t, phit, cs, parent, octant):
    nd, _, _, tl, pc = incoming.shape
    n = parent.shape[0]
    rows, lanes = theta2t.shape[0], phit.shape[1]
    group = 4
    return pl.pallas_call(
        functools.partial(spread_down_kernel, group),
        grid_spec=pltpu.PrefetchScalarGridSpec(
            num_scalar_prefetch=2,
            grid=(n // group,),
            in_specs=[
                pl.BlockSpec(incoming.shape, lambda i, *_: (0, 0, 0, 0, 0)),
                pl.BlockSpec(theta2t.shape, lambda i, *_: (0, 0)),
                pl.BlockSpec(phit.shape, lambda i, *_: (0, 0)),
                pl.BlockSpec(cs.shape, lambda i, *_: (0, 0, 0, 0, 0)),
            ],
            out_specs=pl.BlockSpec((group, rows, lanes), lambda i, *_: (i, 0, 0)),
            scratch_shapes=[pltpu.VMEM((group, 2 * nd * tl, pc), F32)],
        ),
        out_shape=jax.ShapeDtypeStruct((n, rows, lanes), F32),
        compiler_params=pltpu.CompilerParams(vmem_limit_bytes=VMEM_BYTES),
    )(parent, octant, incoming, theta2t, phit, cs)


def shards(
    fine_out,
    theta_interp,
    phi_interp,
    shift_phase,
    translation,
    upper_in,
    children,
    far_boxes,
    far_offsets,
):
    n = fine_out.shape[0]
    tc, tf = theta_interp.shape
    pc = phi_interp.shape[1]
    parents = children.shape[0]
    tl = shift_phase.shape[1] // pc
    nd = tc // tl
    flat = (children % (n * nd)).reshape(-1)
    own = lax.axis_index("dir") * n + jnp.arange(n, dtype=jnp.int32)
    slots = jnp.arange(flat.shape[0], dtype=jnp.int32)
    slot = jnp.sum(jnp.where(flat[None, :] == own[:, None], slots[None, :], 0), axis=1)
    parent, octant = slot // 8, slot % 8
    theta2 = (jnp.eye(2, dtype=F32)[:, None, None, :] * theta_interp[None, :, :, None]).reshape(
        2 * tc, 2 * tf
    )
    phase = shift_phase.reshape(8, tl, pc)
    cs = lax.all_gather(jnp.stack([jnp.cos(phase), jnp.sin(phase)]), "dir", axis=0)
    partial = gather_up(rows_view(fine_out), theta2, phi_interp, cs, parent, octant, parents)
    outgoing = lax.psum_scatter(
        partial.reshape(nd * parents * 2, tl, pc), "dir", scatter_dimension=0, tiled=True
    )
    every_box = lax.all_gather(outgoing.reshape(parents, 2, tl, pc), "box", axis=0, tiled=True)
    rows, planes = translate(
        every_box, rows_view(translation), rows_view(upper_in), far_boxes, far_offsets
    )
    incoming = lax.all_gather(planes, "dir", axis=0)
    fine_in = spread_down(incoming, theta2.T, phi_interp.T, cs, parent, octant)
    return (rows_unview(rows), rows_unview(fine_in))


def solution(mesh):
    placed = (
        P(("box", "dir"), None, None),
        P(),
        P(),
        P(None, "dir"),
        P(None, None, "dir"),
        P("box", None, "dir"),
        P("box", None),
        P("box", None),
        P("box", None),
    )
    return jax.shard_map(
        shards,
        mesh=mesh,
        in_specs=placed,
        out_specs=(P("box", None, "dir"), P(("box", "dir"), None, None)),
        check_vma=False,
    )
```

time: 981 us -> 327 us (0.33); the launches traced: 970 us -> 326 us
  local copies, waits for them, and re-layouts: 414 us -> 2.41 us
  blocking collectives: 188 us -> 0 us
  other arithmetic: 133 us -> 2.59 us
  waiting for transfers between devices: 183 us -> 260 us
  Pallas kernels: 0 us -> 47 us
  matrix products: 30.9 us -> 0 us
    all_to_all x1 -> x0, blocking collectives: 188 us -> none  [shards(): lax.all_to_all(child_in, 'dir', split_axis=0, concat_axis=2, tiled=True)]
    all_gather x1 -> x3, waiting for transfers between devices: 0.01 us -> 184 us  [the longest x1 80.8 us: shards(): incoming = lax.all_gather(planes, 'dir', axis=0)]
    all_to_all x1 -> x0, waiting for transfers between devices: 183 us -> none  [shards(): lax.all_to_all(child_rows, 'dir', split_axis=2, concat_axis=0, tiled=True)]
    gather x6 -> x0, local copies, waits for them, and re-layouts: 123 us -> none  [the longest x1 45.4 us: translate(): kernel_rows = operators[far_kind]]
    unnamed x20 -> x8, local copies, waits for them, and re-layouts: 102 us -> 0.11 us
    reduce_sum x2 -> x1, other arithmetic: 82.9 us -> 0.18 us  [shards(): jnp.sum(jnp.where(flat[None, :] == own[:, None], slots[None, :], 0), axis=1)]
    reduce_scatter x0 -> x1, waiting for transfers between devices: none -> 75.6 us  [shards(): lax.psum_scatter(partial.reshape(nd * parents * 2, tl, pc), 'dir', scatte...]
    all_to_all x5 -> x0, local copies, waits for them, and re-layouts: 74.1 us -> none  [the longest x4 60.3 us: shards(): lax.all_to_all(child_rows, 'dir', split_axis=2, concat_axis=0, tiled=True)]
  transfers between devices with their start and end apart: 2 -> 4, of which waited for: 1 -> 4; matrix products, arithmetic and copies ran while one was open for 6% -> 1% of each run, Pallas kernels for 0% -> 0%
where the time goes in v1:
time: 327 us; the launch traced here: 326 us
  waiting for transfers between devices  260 us (80%)
  Pallas kernels  47 us (14%)
  between operations  13.9 us (4%)
    all_gather x1, waiting for transfers between devices, shards(): incoming = lax.all_gather(planes, 'dir', axis=0)  80.8 us
    reduce_scatter x1, waiting for transfers between devices, shards(): lax.psum_scatter(partial.reshape(nd * parents * 2, tl, pc), 'dir', scatte...  75.6 us
    all_gather x1, waiting for transfers between devices, shards(): lax.all_gather(outgoing.reshape(parents, 2, tl, pc), 'box', axis=0, tiled...  56.9 us
    all_gather x1, waiting for transfers between devices, shards(): lax.all_gather(jnp.stack([jnp.cos(phase), jnp.sin(phase)]), 'dir', axis=0)  46.7 us
    pallas_call x1, Pallas kernels, translate(): pl.pallas_call(translate_kernel, grid_spec=pltpu.PrefetchScalarGridSpec(n...  22.7 us
    pallas_call x1, Pallas kernels, gather_up(): pl.pallas_call(functools.partial(gather_up_kernel, group), grid_spec=pltp...  14.1 us
    pallas_call x1, Pallas kernels, spread_down(): pl.pallas_call(functools.partial(spread_down_kernel, group), grid_spec=pl...  10.2 us
  transfers between devices with their start and end apart: 4, of which 4 were waited for; matrix products, arithmetic and copies ran while one was open for 1% of the time, Pallas kernels for 0%

profile of v1, /device:TPU:0, one launch (start us, length us, event | category | flops | bytes accessed | tf_op | source)
XLA Modules:
  0.0 326.0 jit_solution(18014625039780050120)
XLA Ops:
  7.2 0.0 copy-start
  7.2 0.0 all-gather.8.cloned.1.call-start
  7.2 1.9 fusion.2
  9.1 0.2 copy_bitcast_fusion
  9.3 0.8 pad_maximum_fusion
  10.1 0.0 all-gather.8.cloned.1.call-update
  10.1 0.0 reduce-scatter.2.cloned.1.call-start
  10.2 0.7 add_select_fusion
  10.9 0.1 copy.39
  11.0 0.1 eq.26
  11.1 0.9 broadcast_multiply_fusion
  12.0 0.1 copy.41.theta_ref
  12.1 0.2 select_reduce_fusion
  12.3 46.7 %all-gather.8.cloned.1.call-done = f32[8,8,32,256]{3,2,1,0:T(8,128)} async-done(((f32[2,8,32,256]{3,2,1,0:T(8,128)}), f32[8,8,32,256]{3,2,1,0:T(8,128)}) %all-gather.8.cloned.1.call-update) | async-done | bytes 2097168 | tf_op jit(solution)/shard_map/all_gather | solution.py:219
  58.9 0.0 copy-done
  58.9 14.1 %shard_map.104 = f32[4,16,2,32,256]{4,3,2,1,0:T(8,128)} custom-call(s32[32]{0:T(128)S(1)} %get-tuple-element.11.parent, s32[32]{0:T(128)S(1)} %get-tuple-element.10.octant, f32[32,128,128]{2,1,0:T(8,128)} %bitcast.58, f32[256,128]{1,0:T(8,128)S(1)} %copy.41.theta_ref, f32[128,256]{1,0:T(8,128)S(1)} %copy-done, f32[4,2,8,32,256]{4,3,2,1,0:T(8,128)} %bitcast.55), custom_call_target="tpu_custom_call" | custom-call | tf_op jit(solution)/shard_map/pallas_call | solution.py:63
  73.1 0.0 copy-start.1
  73.1 0.0 copy-start.2
  73.1 0.0 reduce-scatter.2.cloned.1.call-update
  73.1 0.0 all-gather.6.cloned.1.call-start
  73.1 75.6 %reduce-scatter.2.cloned.1.call-done = f32[32,32,256]{2,1,0:T(8,128)} async-done(((f32[128,32,256]{2,1,0:T(8,128)}), f32[32,32,256]{2,1,0:T(8,128)}) %reduce-scatter.2.cloned.1.call-update) | async-done | bytes 1048592 | tf_op jit(solution)/shard_map/reduce_scatter | solution.py:221
  148.7 0.0 all-gather.6.cloned.1.call-update
  148.7 0.0 all-gather.10.cloned.1.call-start
  148.8 56.9 %all-gather.6.cloned.1.call-done.q_ref = f32[128,2,32,256]{3,2,1,0:T(8,128)} async-done(((f32[16,2,32,256]{3,2,1,0:T(8,128)}), f32[128,2,32,256]{3,2,1,0:T(8,128)}) %all-gather.6.cloned.1.call-update) | async-done | bytes 8388624 | tf_op jit(solution)/shard_map/all_gather | solution.py:224
  205.7 0.0 copy-done.1
  205.7 0.0 copy-done.2
  205.7 22.7 %shard_map.105 = (f32[16,128,128]{2,1,0:T(8,128)}, f32[16,2,32,256]{3,2,1,0:T(8,128)}) custom-call(s32[16,28]{1,0:T(8,128)S(1)} %copy-done.1, s32[16,28]{1,0:T(8,128)S(1)} %copy-done.2, f32[128,2,32,256]{3,2,1,0:T(8,128)} %all-gather.6.cloned.1.call-done.q_ref, f32[316,128,128]{2,1,0:T(8,128)} %bitcast.53, f32[16,128,128]{2,1,0:T(8,128)} %bitcast.60), custom_call_target="tpu_custom_call" | custom-call | tf_op jit(solution)/shard_map/pallas_call | solution.py:123
  228.4 0.0 all-gather.10.cloned.1.call-update
  228.4 0.1 copy.45
  228.5 80.8 %all-gather.10.cloned.1.call-done = f32[64,2,32,256]{3,2,1,0:T(8,128)} async-done(((f32[16,2,32,256]{3,2,1,0:T(8,128)}), f32[64,2,32,256]{3,2,1,0:T(8,128)}) %all-gather.10.cloned.1.call-update) | async-done | bytes 4194320 | tf_op jit(solution)/shard_map/all_gather | solution.py:228
  309.3 10.2 %shard_map.106 = f32[32,128,128]{2,1,0:T(8,128)} custom-call(s32[32]{0:T(128)S(1)} %get-tuple-element.11.parent, s32[32]{0:T(128)S(1)} %get-tuple-element.10.octant, f32[4,16,2,32,256]{4,3,2,1,0:T(8,128)} %bitcast.57, f32[128,256]{1,0:T(8,128)S(1)} %bitcast.51, f32[256,128]{1,0:T(8,128)S(1)} %bitcast.52, f32[4,2,8,32,256]{4,3,2,1,0:T(8,128)} %bitcast.56), custom_call_target="tpu_custom_call" | custom-call | tf_op jit(solution)/shard_map/pallas_call | solution.py:174
  (4 shorter events, 0.0 us)
Async XLA Ops:
  7.2 51.8 %copy-start = (f32[128,256]{1,0:T(8,128)S(1)}, f32[128,256]{1,0:T(8,128)}, u32[]{:S(2)}) copy-start(f32[128,256]{1,0:T(8,128)} %phi_ref.1) | copy-start | bytes 393220
  7.2 51.8 %all-gather.8.cloned.1.call-start = ((), (), s32[]{:S(2)}) async-start(), calls=%async_computation.3 | async-start | bytes 2621440 | tf_op jit(solution)/shard_map/all_gather | solution.py:219
  10.1 138.6 %reduce-scatter.2.cloned.1.call-start = ((), (), s32[]{:S(2)}) async-start(), calls=%async_computation.1 | async-start | bytes 5242880 | tf_op jit(solution)/shard_map/reduce_scatter | solution.py:221
  73.1 132.7 %copy-start.1 = (s32[16,28]{1,0:T(8,128)S(1)}, s32[16,28]{1,0:T(8,128)}, u32[]{:S(2)}) copy-start(s32[16,28]{1,0:T(8,128)} %far.1) | copy-start | bytes 5380
  73.1 132.7 %copy-start.2 = (s32[16,28]{1,0:T(8,128)S(1)}, s32[16,28]{1,0:T(8,128)}, u32[]{:S(2)}) copy-start(s32[16,28]{1,0:T(8,128)} %kind.1) | copy-start | bytes 5380
  73.1 132.6 %all-gather.6.cloned.1.call-start = ((), (), s32[]{:S(2)}) async-start(), calls=%async_computation.2 | async-start | bytes 9437184 | tf_op jit(solution)/shard_map/all_gather | solution.py:224
  148.7 160.6 %all-gather.10.cloned.1.call-start = ((), (), s32[]{:S(2)}) async-start(), calls=%async_computation.4 | async-start | bytes 5242880 | tf_op jit(solution)/shard_map/all_gather | solution.py:228
Sparse Core Ops, SparseCore 0:
  10.3 48.6 all-gather.7
  73.2 75.4 reduce-scatter.1
  150.8 54.8 all-gather.5
  228.6 80.6 all-gather.9

commit v2 on v1

--- a/solution.py
+++ b/solution.py
@@ -9,6 +9,7 @@
 
 F32, BF16 = jnp.float32, jnp.bfloat16
 VMEM_BYTES = 52 * 1024 * 1024
+CHUNKS = 2
 
 
 def split(x):
@@ -32,14 +33,16 @@
     return x.reshape(n, r // 2, 2, 128).transpose(0, 2, 1, 3).reshape(n, 2, r * 64)
 
 
-def gather_up_kernel(group, parent, octant, x_ref, theta_ref, phi_ref, cs_ref, out_ref):
+def gather_up_kernel(group, parent, octant, x_ref, theta_ref, phi_ref, cs_ref, *out_refs):
     step = pl.program_id(0)
-    nd, tl = out_ref.shape[0], out_ref.shape[3]
+    nd, tl = cs_ref.shape[0], cs_ref.shape[3]
+    tlc = tl // len(out_refs)
     tc = nd * tl
 
     @pl.when(step == 0)
     def _():
-        out_ref[...] = jnp.zeros_like(out_ref)
+        for out_ref in out_refs:
+            out_ref[...] = jnp.zeros_like(out_ref)
 
     theta = split(theta_ref[...])
     phi = split(phi_ref[...])
@@ -49,16 +52,20 @@
         p, o = parent[step * group + g], octant[step * group + g]
         full = dot3(theta, split(along[g * rows : (g + 1) * rows]))
         for j in range(nd):
-            re = full[j * tl : (j + 1) * tl]
-            im = full[tc + j * tl : tc + (j + 1) * tl]
-            c, s = cs_ref[j, 0, o], cs_ref[j, 1, o]
-            out_ref[j, p, 0] += c * re - s * im
-            out_ref[j, p, 1] += s * re + c * im
+            for h, out_ref in enumerate(out_refs):
+                first = j * tl + h * tlc
+                re = full[first : first + tlc]
+                im = full[tc + first : tc + first + tlc]
+                c = cs_ref[j, 0, o, h * tlc : (h + 1) * tlc]
+                s = cs_ref[j, 1, o, h * tlc : (h + 1) * tlc]
+                out_ref[j, p, 0] += c * re - s * im
+                out_ref[j, p, 1] += s * re + c * im
 
 
 def gather_up(x, theta2, phi, cs, parent, octant, parents):
     n, rows, lanes = x.shape
     nd, _, _, tl, pc = cs.shape
+    shape = (nd, parents, 2, tl // CHUNKS, pc)
     group = 4
     return pl.pallas_call(
         functools.partial(gather_up_kernel, group),
@@ -71,21 +78,25 @@
                 pl.BlockSpec(phi.shape, lambda i, *_: (0, 0)),
                 pl.BlockSpec(cs.shape, lambda i, *_: (0, 0, 0, 0, 0)),
             ],
-            out_specs=pl.BlockSpec((nd, parents, 2, tl, pc), lambda i, *_: (0, 0, 0, 0, 0)),
+            out_specs=[pl.BlockSpec(shape, lambda i, *_: (0, 0, 0, 0, 0))] * CHUNKS,
         ),
-        out_shape=jax.ShapeDtypeStruct((nd, parents, 2, tl, pc), F32),
+        out_shape=[jax.ShapeDtypeStruct(shape, F32)] * CHUNKS,
         compiler_params=pltpu.CompilerParams(vmem_limit_bytes=VMEM_BYTES),
     )(parent, octant, x, theta2, phi, cs)
 
 
-def translate_kernel(far, kind, q_ref, trans_ref, upper_ref, rows_ref, plane_ref, buf, sem):
+def translate_kernel(chunk, far, kind, q_ref, trans_ref, upper_ref, *refs):
+    rows_ref, plane_ref, buf, sem = refs[-4:]
     p = pl.program_id(0)
     count, many = pl.num_programs(0), far.shape[1]
     tl = q_ref.shape[2]
+    part = pl.ds(chunk * buf.shape[2], buf.shape[2])
 
     def start(row, slot):
         for l in range(many):
-            pltpu.make_async_copy(trans_ref.at[kind[row, l]], buf.at[slot, l], sem.at[slot]).start()
+            pltpu.make_async_copy(
+                trans_ref.at[kind[row, l], part], buf.at[slot, l], sem.at[slot]
+            ).start()
 
     @pl.when(p == 0)
     def _():
@@ -96,7 +107,7 @@
         start(p + 1, (p + 1) % 2)
 
     slot = p % 2
-    pltpu.make_async_copy(trans_ref.at[pl.ds(0, many)], buf.at[slot], sem.at[slot]).wait()
+    pltpu.make_async_copy(trans_ref.at[pl.ds(0, many), part], buf.at[slot], sem.at[slot]).wait()
     for t in range(0, tl, 8):
         for h in range(2):
             re = im = None
@@ -116,22 +127,24 @@
                 plane_ref[0, c, t : t + 8, h * 128 : (h + 1) * 128] = total
 
 
-def translate(q, trans, upper, far, kind):
-    parents, rows, lanes = upper.shape
+def translate(chunk, q, trans, upper, far, kind, before):
+    parents, all_rows, lanes = upper.shape
+    rows = all_rows // CHUNKS
     _, _, tl, pc = q.shape
     many = far.shape[1]
     return pl.pallas_call(
-        translate_kernel,
+        functools.partial(translate_kernel, chunk),
         grid_spec=pltpu.PrefetchScalarGridSpec(
             num_scalar_prefetch=2,
             grid=(parents,),
             in_specs=[
                 pl.BlockSpec(q.shape, lambda i, *_: (0, 0, 0, 0)),
                 pl.BlockSpec(memory_space=pl.ANY),
-                pl.BlockSpec((1, rows, lanes), lambda i, *_: (i, 0, 0)),
-            ],
+                pl.BlockSpec((1, rows, lanes), lambda i, *_: (i, chunk, 0)),
+            ]
+            + [pl.BlockSpec(memory_space=pl.ANY)] * len(before),
             out_specs=[
-                pl.BlockSpec((1, rows, lanes), lambda i, *_: (i, 0, 0)),
+                pl.BlockSpec((1, rows, lanes), lambda i, *_: (i, chunk, 0)),
                 pl.BlockSpec((1, 2, tl, pc), lambda i, *_: (i, 0, 0, 0)),
             ],
             scratch_shapes=[
@@ -140,16 +153,19 @@
             ],
         ),
         out_shape=[
-            jax.ShapeDtypeStruct((parents, rows, lanes), F32),
+            jax.ShapeDtypeStruct((parents, all_rows, lanes), F32),
             jax.ShapeDtypeStruct((parents, 2, tl, pc), F32),
         ],
         compiler_params=pltpu.CompilerParams(vmem_limit_bytes=VMEM_BYTES),
-    )(far, kind, q, trans, upper)
-
-
-def spread_down_kernel(group, parent, octant, in_ref, theta_ref, phi_ref, cs_ref, out_ref, full):
+        input_output_aliases={5: 0} if before else {},
+    )(far, kind, q, trans, upper, *before)
+
+
+def spread_down_kernel(group, parent, octant, *refs):
+    in_refs, (theta_ref, phi_ref, cs_ref, out_ref, full) = refs[:-5], refs[-5:]
     step = pl.program_id(0)
-    nd, tl = in_ref.shape[0], in_ref.shape[3]
+    nd, tl = cs_ref.shape[0], cs_ref.shape[3]
+    tlc = tl // len(in_refs)
     tc = nd * tl
     theta = split(theta_ref[...])
     phi = split(phi_ref[...])
@@ -157,17 +173,20 @@
     for g in range(group):
         p, o = parent[step * group + g], octant[step * group + g]
         for j in range(nd):
-            re, im = in_ref[j, p, 0], in_ref[j, p, 1]
-            c, s = cs_ref[j, 0, o], cs_ref[j, 1, o]
-            full[g, j * tl : (j + 1) * tl] = c * re + s * im
-            full[g, tc + j * tl : tc + (j + 1) * tl] = c * im - s * re
+            for h, in_ref in enumerate(in_refs):
+                first = j * tl + h * tlc
+                re, im = in_ref[j, p, 0], in_ref[j, p, 1]
+                c = cs_ref[j, 0, o, h * tlc : (h + 1) * tlc]
+                s = cs_ref[j, 1, o, h * tlc : (h + 1) * tlc]
+                full[g, first : first + tlc] = c * re + s * im
+                full[g, tc + first : tc + first + tlc] = c * im - s * re
         parts.append(dot3(theta, split(full[g])))
     along = jnp.concatenate(parts, axis=0)
     out_ref[...] = dot3(split(along), phi).reshape(out_ref.shape)
 
 
 def spread_down(incoming, theta2t, phit, cs, parent, octant):
-    nd, _, _, tl, pc = incoming.shape
+    nd, _, _, tl, pc = cs.shape
     n = parent.shape[0]
     rows, lanes = theta2t.shape[0], phit.shape[1]
     group = 4
@@ -177,7 +196,7 @@
             num_scalar_prefetch=2,
             grid=(n // group,),
             in_specs=[
-                pl.BlockSpec(incoming.shape, lambda i, *_: (0, 0, 0, 0, 0)),
+                *(pl.BlockSpec(x.shape, lambda i, *_: (0, 0, 0, 0, 0)) for x in incoming),
                 pl.BlockSpec(theta2t.shape, lambda i, *_: (0, 0)),
                 pl.BlockSpec(phit.shape, lambda i, *_: (0, 0)),
                 pl.BlockSpec(cs.shape, lambda i, *_: (0, 0, 0, 0, 0)),
@@ -187,7 +206,7 @@
         ),
         out_shape=jax.ShapeDtypeStruct((n, rows, lanes), F32),
         compiler_params=pltpu.CompilerParams(vmem_limit_bytes=VMEM_BYTES),
-    )(parent, octant, incoming, theta2t, phit, cs)
+    )(parent, octant, *incoming, theta2t, phit, cs)
 
 
 def shards(
@@ -215,17 +234,31 @@
     theta2 = (jnp.eye(2, dtype=F32)[:, None, None, :] * theta_interp[None, :, :, None]).reshape(
         2 * tc, 2 * tf
     )
-    phase = shift_phase.reshape(8, tl, pc)
-    cs = lax.all_gather(jnp.stack([jnp.cos(phase), jnp.sin(phase)]), "dir", axis=0)
-    partial = gather_up(rows_view(fine_out), theta2, phi_interp, cs, parent, octant, parents)
-    outgoing = lax.psum_scatter(
-        partial.reshape(nd * parents * 2, tl, pc), "dir", scatter_dimension=0, tiled=True
-    )
-    every_box = lax.all_gather(outgoing.reshape(parents, 2, tl, pc), "box", axis=0, tiled=True)
-    rows, planes = translate(
-        every_box, rows_view(translation), rows_view(upper_in), far_boxes, far_offsets
-    )
-    incoming = lax.all_gather(planes, "dir", axis=0)
+    nb = lax.axis_size("box")
+    phase = shift_phase.reshape(8 * tl, pc)
+    share = 8 * tl // nb
+    mine = lax.dynamic_slice_in_dim(phase, lax.axis_index("box") * share, share, axis=0)
+    phases = lax.all_gather(mine, ("box", "dir"), axis=0, tiled=False)
+    phases = phases.reshape(nb, nd, share, pc).transpose(1, 0, 2, 3).reshape(nd, 8, tl, pc)
+    cs = jnp.stack([jnp.cos(phases), jnp.sin(phases)], axis=1)
+    partials = gather_up(rows_view(fine_out), theta2, phi_interp, cs, parent, octant, parents)
+    operators, upper = rows_view(translation), rows_view(upper_in)
+    every_box = []
+    for partial in partials:
+        outgoing = lax.psum_scatter(
+            partial.reshape((nd * parents * 2,) + partial.shape[3:]),
+            "dir",
+            scatter_dimension=0,
+            tiled=True,
+        ).reshape(partial.shape[1:])
+        every_box.append(lax.all_gather(outgoing, "box", axis=0, tiled=True))
+    before, incoming = (), []
+    for chunk, sources in enumerate(every_box):
+        rows, planes = translate(
+            chunk, sources, operators, upper, far_boxes, far_offsets, before
+        )
+        before = (rows,)
+        incoming.append(lax.all_gather(planes, "dir", axis=0))
     fine_in = spread_down(incoming, theta2.T, phi_interp.T, cs, parent, octant)
     return (rows_unview(rows), rows_unview(fine_in))
 

time: 327 us -> 383 us (1.17)
  waiting for transfers between devices: 260 us -> 299 us
  Pallas kernels: 47 us -> 56.3 us
  local copies, waits for them, and re-layouts: 2.41 us -> 6.89 us
    all_gather x3 -> x5, waiting for transfers between devices: 184 us -> 210 us  [the longest x2 92.3 us: shards(): incoming.append(lax.all_gather(planes, 'dir', axis=0))]
    reduce_scatter x1 -> x2, waiting for transfers between devices: 75.6 us -> 87.7 us  [shards(): lax.psum_scatter(partial.reshape((nd * parents * 2,) + partial.shape[3:])...]
    pallas_call x1 -> x2, Pallas kernels: 22.7 us -> 31.7 us  [translate(): pl.pallas_call(functools.partial(translate_kernel, chunk), grid_spec=pltp...]
  transfers between devices with their start and end apart: 4 -> 7, of which waited for: 4 -> 7; matrix products, arithmetic and copies ran while one was open for 1% -> 1% of each run, Pallas kernels for 0% -> 4%
where the time goes in v2:
time: 383 us; the launch traced here: 380 us
  waiting for transfers between devices  299 us (78%)
  Pallas kernels  56.3 us (15%)
  between operations  14.3 us (4%)
  local copies, waits for them, and re-layouts  6.89 us (2%)
    all_gather x2, waiting for transfers between devices, shards(): incoming.append(lax.all_gather(planes, 'dir', axis=0))  92.3 us
    reduce_scatter x2, waiting for transfers between devices, shards(): lax.psum_scatter(partial.reshape((nd * parents * 2,) + partial.shape[3:])...  87.7 us
    all_gather x2, waiting for transfers between devices, shards(): every_box.append(lax.all_gather(outgoing, 'box', axis=0, tiled=True))  60.2 us
    all_gather x1, waiting for transfers between devices, shards(): phases = lax.all_gather(mine, ('box', 'dir'), axis=0, tiled=False)  57.1 us
    pallas_call x2, Pallas kernels, translate(): pl.pallas_call(functools.partial(translate_kernel, chunk), grid_spec=pltp...  31.7 us
    pallas_call x1, Pallas kernels, gather_up(): pl.pallas_call(functools.partial(gather_up_kernel, group), grid_spec=pltp...  14.4 us
    pallas_call x1, Pallas kernels, spread_down(): pl.pallas_call(functools.partial(spread_down_kernel, group), grid_spec=pl...  10.3 us
  transfers between devices with their start and end apart: 7, of which 7 were waited for; matrix products, arithmetic and copies ran while one was open for 1% of the time, Pallas kernels for 4%

profile of v2, /device:TPU:0, one launch (start us, length us, event | category | flops | bytes accessed | tf_op | source)
XLA Modules:
  0.0 379.9 jit_solution(1578368925350440274)
XLA Ops:
  7.2 0.0 all-gather.13.cloned.1.call-start
  7.2 1.0 reshape.72
  8.2 0.6 constant_dynamic-slice_fusion
  8.9 0.0 reduce-scatter.5.cloned.1.call-start
  8.9 0.7 add_select_fusion
  9.6 0.1 copy.40
  9.7 0.1 eq.26
  9.8 0.9 broadcast_multiply_fusion
  10.7 0.1 copy.44.theta_ref
  10.8 0.2 select_reduce_fusion
  11.0 57.1 %all-gather.13.cloned.1.call-done = f32[1024,256]{1,0:T(8,128)} async-done(((f32[32,256]{1,0:T(8,128)}), f32[1024,256]{1,0:T(8,128)}) %all-gather.13.cloned.1.call-update) | async-done | bytes 1048592 | tf_op jit(solution)/shard_map/all_gather | solution.py:241
  68.0 4.7 %fusion.2 = (f32[1024,256]{1,0:T(8,128)S(1)}, f32[1024,256]{1,0:T(8,128)S(1)}) fusion(f32[1024,256]{1,0:T(8,128)} %all-gather.13.cloned.1.call-done), kind=kLoop, calls=%fused_computation.19 | loop fusion | bytes 3145728 | tf_op jit(solution)/shard_map/cos | solution.py:243
  72.7 0.2 copy_bitcast_fusion
  73.0 1.5 pad_maximum_fusion.cs_ref.refs_4_
  74.5 14.4 %shard_map.104 = (f32[4,16,2,16,256]{4,3,2,1,0:T(8,128)}, f32[4,16,2,16,256]{4,3,2,1,0:T(8,128)}) custom-call(s32[32]{0:T(128)S(1)} %get-tuple-element.19.parent, s32[32]{0:T(128)S(1)} %get-tuple-element.18.octant, f32[32,128,128]{2,1,0:T(8,128)} %bitcast.66, f32[256,128]{1,0:T(8,128)S(1)} %copy.44.theta_ref, f32[128,256]{1,0:T(8,128)S(1)} %copy-done.1, ...), custom_call_target="tpu_custom_call" | custom-call | tf_op jit(solution)/shard_map/pallas_call | solution.py:70
  89.0 0.0 reduce-scatter.3.cloned.1.call-start
  89.0 0.7 reduce-scatter.3.cloned.1.call-update
  89.7 0.0 all-gather.11.cloned.1.call-start
  89.7 42.2 %reduce-scatter.5.cloned.1.call-done = f32[32,16,256]{2,1,0:T(8,128)} async-done(((f32[128,16,256]{2,1,0:T(8,128)}), f32[32,16,256]{2,1,0:T(8,128)}) %reduce-scatter.5.cloned.1.call-update) | async-done | bytes 524304 | tf_op jit(solution)/shard_map/reduce_scatter | solution.py:248
  131.9 0.0 all-gather.9.cloned.1.call-start
  132.0 45.6 %reduce-scatter.3.cloned.1.call-done = f32[32,16,256]{2,1,0:T(8,128)} async-done(((f32[128,16,256]{2,1,0:T(8,128)}), f32[32,16,256]{2,1,0:T(8,128)}) %reduce-scatter.3.cloned.1.call-update) | async-done | bytes 524304 | tf_op jit(solution)/shard_map/reduce_scatter | solution.py:248
  177.6 0.0 all-gather.17.cloned.1.call-start
  177.6 37.7 %all-gather.11.cloned.1.call-done.q_ref = f32[128,2,16,256]{3,2,1,0:T(8,128)} async-done(((f32[16,2,16,256]{3,2,1,0:T(8,128)}), f32[128,2,16,256]{3,2,1,0:T(8,128)}) %all-gather.11.cloned.1.call-update) | async-done | bytes 4194320 | tf_op jit(solution)/shard_map/all_gather | solution.py:254
  215.3 16.0 %shard_map.105 = (f32[16,128,128]{2,1,0:T(8,128)}, f32[16,2,16,256]{3,2,1,0:T(8,128)}) custom-call(s32[16,28]{1,0:T(8,128)S(1)} %copy-done.2, s32[16,28]{1,0:T(8,128)S(1)} %copy-done.3, f32[128,2,16,256]{3,2,1,0:T(8,128)} %all-gather.11.cloned.1.call-done.q_ref, f32[316,128,128]{2,1,0:T(8,128)} %bitcast.59, f32[16,128,128]{2,1,0:T(8,128)S(1)} %bitcast.54), custom_call_target="tpu_custom_call" | custom-call | tf_op jit(solution)/shard_map/pallas_call | solution.py:135
  231.3 22.5 %all-gather.9.cloned.1.call-done.q_ref = f32[128,2,16,256]{3,2,1,0:T(8,128)} async-done(((f32[16,2,16,256]{3,2,1,0:T(8,128)}), f32[128,2,16,256]{3,2,1,0:T(8,128)}) %all-gather.9.cloned.1.call-update) | async-done | bytes 4194320 | tf_op jit(solution)/shard_map/all_gather | solution.py:254
  253.8 15.7 %shard_map.106 = (f32[16,128,128]{2,1,0:T(8,128)}, f32[16,2,16,256]{3,2,1,0:T(8,128)}) custom-call(s32[16,28]{1,0:T(8,128)S(1)} %copy-done.2, s32[16,28]{1,0:T(8,128)S(1)} %copy-done.3, f32[128,2,16,256]{3,2,1,0:T(8,128)} %all-gather.9.cloned.1.call-done.q_ref, f32[316,128,128]{2,1,0:T(8,128)} %bitcast.60, ...), custom_call_target="tpu_custom_call", output_to_operand_aliasing={{0}: (5, {})} | custom-call | tf_op jit(solution)/shard_map/pallas_call | solution.py:135
  269.6 0.0 all-gather.15.cloned.1.call-start
  269.6 0.7 all-gather.15.cloned.1.call-update
  270.3 0.1 copy.48
  270.4 45.5 %all-gather.17.cloned.1.call-done = f32[64,2,16,256]{3,2,1,0:T(8,128)} async-done(((f32[16,2,16,256]{3,2,1,0:T(8,128)}), f32[64,2,16,256]{3,2,1,0:T(8,128)}) %all-gather.17.cloned.1.call-update) | async-done | bytes 2097168 | tf_op jit(solution)/shard_map/all_gather | solution.py:261
  315.9 46.8 %all-gather.15.cloned.1.call-done = f32[64,2,16,256]{3,2,1,0:T(8,128)} async-done(((f32[16,2,16,256]{3,2,1,0:T(8,128)}), f32[64,2,16,256]{3,2,1,0:T(8,128)}) %all-gather.15.cloned.1.call-update) | async-done | bytes 2097168 | tf_op jit(solution)/shard_map/all_gather | solution.py:261
  362.8 10.3 %shard_map.107 = f32[32,128,128]{2,1,0:T(8,128)} custom-call(s32[32]{0:T(128)S(1)} %get-tuple-element.19.parent, s32[32]{0:T(128)S(1)} %get-tuple-element.18.octant, f32[4,16,2,16,256]{4,3,2,1,0:T(8,128)} %bitcast.64, f32[4,16,2,16,256]{4,3,2,1,0:T(8,128)} %bitcast.63, f32[128,256]{1,0:T(8,128)S(1)} %bitcast.57, f32[256,128]{1,0:T(8,128)S(1)} %bitcast.58, ...), custom_call_target="tpu_custom_call" | custom-call | tf_op jit(solution)/shard_map/pallas_call | solution.py:193
  (17 shorter events, 0.1 us)
Async XLA Ops:
  7.2 60.9 %all-gather.13.cloned.1.call-start = ((), (), s32[]{:S(2)}) async-start(), calls=%async_computation.6 | async-start | bytes 1081344 | tf_op jit(solution)/shard_map/all_gather | solution.py:241
  8.9 123.0 %reduce-scatter.5.cloned.1.call-start = ((), (), s32[]{:S(2)}) async-start(), calls=%async_computation.4 | async-start | bytes 2621440 | tf_op jit(solution)/shard_map/reduce_scatter | solution.py:248
  73.0 1.5 copy-start.1
  88.9 126.4 %copy-start = (f32[16,2,8192]{2,1,0:T(2,128)S(1)}, f32[16,2,8192]{2,1,0:T(2,128)}, u32[]{:S(2)}) copy-start(f32[16,2,8192]{2,1,0:T(2,128)} %param.14) | copy-start | bytes 3145732
  88.9 126.4 %copy-start.2 = (s32[16,28]{1,0:T(8,128)S(1)}, s32[16,28]{1,0:T(8,128)}, u32[]{:S(2)}) copy-start(s32[16,28]{1,0:T(8,128)} %far.3) | copy-start | bytes 5380
  88.9 126.4 %copy-start.3 = (s32[16,28]{1,0:T(8,128)S(1)}, s32[16,28]{1,0:T(8,128)}, u32[]{:S(2)}) copy-start(s32[16,28]{1,0:T(8,128)} %kind.3) | copy-start | bytes 5380
  89.0 88.6 %reduce-scatter.3.cloned.1.call-start = ((), (), s32[]{:S(2)}) async-start(), calls=%async_computation.2 | async-start | bytes 2621440 | tf_op jit(solution)/shard_map/reduce_scatter | solution.py:248
  89.7 125.6 %all-gather.11.cloned.1.call-start = ((), (), s32[]{:S(2)}) async-start(), calls=%async_computation.5 | async-start | bytes 4718592 | tf_op jit(solution)/shard_map/all_gather | solution.py:254
  131.9 121.9 %all-gather.9.cloned.1.call-start = ((), (), s32[]{:S(2)}) async-start(), calls=%async_computation.3 | async-start | bytes 4718592 | tf_op jit(solution)/shard_map/all_gather | solution.py:254
  177.6 138.4 %all-gather.17.cloned.1.call-start = ((), (), s32[]{:S(2)}) async-start(), calls=%async_computation.8 | async-start | bytes 2621440 | tf_op jit(solution)/shard_map/all_gather | solution.py:261
  269.6 93.2 %all-gather.15.cloned.1.call-start = ((), (), s32[]{:S(2)}) async-start(), calls=%async_computation.7 | async-start | bytes 2621440 | tf_op jit(solution)/shard_map/all_gather | solution.py:261
Sparse Core Ops, SparseCore 0:
  11.6 56.4 all-gather.12
  89.0 42.8 reduce-scatter.4
  134.3 43.1 reduce-scatter.2
  179.3 36.0 all-gather.10
  217.1 36.7 all-gather.8
  269.7 46.1 all-gather.16
  318.1 44.6 all-gather.14

commit v3 on v2

--- a/solution.py
+++ b/solution.py
@@ -209,6 +209,26 @@
     )(parent, octant, *incoming, theta2t, phit, cs)
 
 
+def box_bits():
+    return range(lax.axis_size("box").bit_length() - 2, -1, -1)
+
+
+def gather_box(x):
+    nb = lax.axis_size("box")
+    for bit in box_bits():
+        other = lax.ppermute(x, "box", [(i, i ^ (1 << bit)) for i in range(nb)])
+        x = jnp.concatenate([x, other], axis=0)
+    return x
+
+
+def box_place(box):
+    apart = box ^ lax.axis_index("box")
+    place = jnp.zeros_like(box)
+    for stage, bit in enumerate(box_bits()):
+        place = place + (((apart >> bit) & 1) << stage)
+    return place
+
+
 def shards(
     fine_out,
     theta_interp,
@@ -234,12 +254,7 @@
     theta2 = (jnp.eye(2, dtype=F32)[:, None, None, :] * theta_interp[None, :, :, None]).reshape(
         2 * tc, 2 * tf
     )
-    nb = lax.axis_size("box")
-    phase = shift_phase.reshape(8 * tl, pc)
-    share = 8 * tl // nb
-    mine = lax.dynamic_slice_in_dim(phase, lax.axis_index("box") * share, share, axis=0)
-    phases = lax.all_gather(mine, ("box", "dir"), axis=0, tiled=False)
-    phases = phases.reshape(nb, nd, share, pc).transpose(1, 0, 2, 3).reshape(nd, 8, tl, pc)
+    phases = lax.all_gather(shift_phase.reshape(8, tl, pc), "dir", axis=0)
     cs = jnp.stack([jnp.cos(phases), jnp.sin(phases)], axis=1)
     partials = gather_up(rows_view(fine_out), theta2, phi_interp, cs, parent, octant, parents)
     operators, upper = rows_view(translation), rows_view(upper_in)
@@ -251,11 +266,14 @@
             scatter_dimension=0,
             tiled=True,
         ).reshape(partial.shape[1:])
-        every_box.append(lax.all_gather(outgoing, "box", axis=0, tiled=True))
+        if every_box:
+            every_box[-1], outgoing = lax.optimization_barrier((every_box[-1], outgoing))
+        every_box.append(gather_box(outgoing))
+    sources_at = box_place(far_boxes // parents) * parents + far_boxes % parents
     before, incoming = (), []
     for chunk, sources in enumerate(every_box):
         rows, planes = translate(
-            chunk, sources, operators, upper, far_boxes, far_offsets, before
+            chunk, sources, operators, upper, sources_at, far_offsets, before
         )
         before = (rows,)
         incoming.append(lax.all_gather(planes, "dir", axis=0))

time: 383 us -> 296 us (0.77)
  waiting for transfers between devices: 299 us -> 198 us
  other arithmetic: 3.29 us -> 11.9 us
  starting transfers between devices: 0.28 us -> 6.37 us
    all_gather x3 -> x1, waiting for transfers between devices: 117 us -> 29.7 us  [shards(): phases = lax.all_gather(shift_phase.reshape(8, tl, pc), 'dir', axis=0)]
    ppermute x0 -> x6, waiting for transfers between devices: none -> 63 us  [gather_box(): other = lax.ppermute(x, 'box', [(i, i ^ 1 << bit) for i in range(nb)])]
    reduce_scatter x2, waiting for transfers between devices: 87.7 us -> 42.7 us  [shards(): lax.psum_scatter(partial.reshape((nd * parents * 2,) + partial.shape[3:])...]
    all_gather x2, waiting for transfers between devices: 92.3 us -> 61.6 us  [shards(): incoming.append(lax.all_gather(planes, 'dir', axis=0))]
    concatenate x0 -> x6, other arithmetic: none -> 8.62 us  [gather_box(): x = jnp.concatenate([x, other], axis=0)]
    ppermute x0 -> x6, starting transfers between devices: none -> 6.17 us  [gather_box(): other = lax.ppermute(x, 'box', [(i, i ^ 1 << bit) for i in range(nb)])]
    cos x1 -> x0, local copies, waits for them, and re-layouts: 4.66 us -> none  [shards(): cs = jnp.stack([jnp.cos(phases), jnp.sin(phases)], axis=1)]
    another operation x1, local copies, waits for them, and re-layouts: 0.24 us -> 4.66 us  [shards(): cs = jnp.stack([jnp.cos(phases), jnp.sin(phases)], axis=1)]
  transfers between devices with their start and end apart: 7 -> 11, of which waited for: 7 -> 10; matrix products, arithmetic and copies ran while one was open for 1% -> 3% of each run, Pallas kernels for 4% -> 11%
where the time goes in v3:
time: 296 us; the launch traced here: 293 us
  waiting for transfers between devices  198 us (67%)
  Pallas kernels  56.1 us (19%)
  between operations  13.9 us (5%)
  other arithmetic  11.9 us (4%)
  local copies, waits for them, and re-layouts  6.77 us (2%)
  starting transfers between devices  6.37 us (2%)
    ppermute x6, waiting for transfers between devices, gather_box(): other = lax.ppermute(x, 'box', [(i, i ^ 1 << bit) for i in range(nb)])  63 us
    all_gather x2, waiting for transfers between devices, shards(): incoming.append(lax.all_gather(planes, 'dir', axis=0))  61.6 us
    reduce_scatter x2, waiting for transfers between devices, shards(): lax.psum_scatter(partial.reshape((nd * parents * 2,) + partial.shape[3:])...  42.7 us
    pallas_call x2, Pallas kernels, translate(): pl.pallas_call(functools.partial(translate_kernel, chunk), grid_spec=pltp...  31.4 us
    all_gather x1, waiting for transfers between devices, shards(): phases = lax.all_gather(shift_phase.reshape(8, tl, pc), 'dir', axis=0)  29.7 us
    pallas_call x1, Pallas kernels, gather_up(): pl.pallas_call(functools.partial(gather_up_kernel, group), grid_spec=pltp...  14.4 us
    pallas_call x1, Pallas kernels, spread_down(): pl.pallas_call(functools.partial(spread_down_kernel, group), grid_spec=pl...  10.3 us
    concatenate x6, other arithmetic, gather_box(): x = jnp.concatenate([x, other], axis=0)  8.62 us
  transfers between devices with their start and end apart: 11, of which 10 were waited for; matrix products, arithmetic and copies ran while one was open for 3% of the time, Pallas kernels for 11%

profile of v3, /device:TPU:0, one launch (start us, length us, event | category | flops | bytes accessed | tf_op | source)
XLA Modules:
  0.0 292.8 jit_solution(2454090615385272910)
XLA Ops:
  7.2 1.7 copy.52
  9.0 0.7 add_select_fusion.2
  9.9 0.9 broadcast_multiply_fusion
  10.9 0.2 select_reduce_fusion
  11.1 29.7 %all-gather.6.cloned.1.call-done = f32[4,8,32,256]{3,2,1,0:T(8,128)} async-done(((f32[1,8,32,256]{3,2,1,0:T(8,128)}), f32[4,8,32,256]{3,2,1,0:T(8,128)}) %all-gather.6.cloned.1.call-update) | async-done | bytes 1048592 | tf_op jit(solution)/shard_map/all_gather | solution.py:257
  40.8 4.7 %cosine_bitcast_fusion = (f32[4,1,8,32,256]{4,3,2,1,0:T(8,128)S(1)}, f32[4,1,8,32,256]{4,3,2,1,0:T(8,128)S(1)}) fusion(f32[4,8,32,256]{3,2,1,0:T(8,128)} %all-gather.6.cloned.1.call-done), kind=kLoop, calls=%fused_computation.8 | loop fusion | bytes 3145728 | tf_op jit(solution)/shard_map/stack | solution.py:258
  45.5 1.5 pad_maximum_fusion.2.cs_ref.refs_4_
  47.0 14.4 %shard_map.104 = (f32[4,16,2,16,256]{4,3,2,1,0:T(8,128)}, f32[4,16,2,16,256]{4,3,2,1,0:T(8,128)}) custom-call(s32[32]{0:T(128)S(1)} %get-tuple-element.23.parent, s32[32]{0:T(128)S(1)} %get-tuple-element.22.octant, f32[32,128,128]{2,1,0:T(8,128)} %bitcast.71, f32[256,128]{1,0:T(8,128)S(1)} %copy.40.theta_ref, f32[128,256]{1,0:T(8,128)S(1)} %copy-done.1, ...), custom_call_target="tpu_custom_call" | custom-call | tf_op jit(solution)/shard_map/pallas_call | solution.py:70
  61.5 0.7 reduce-scatter.5.cloned.1.call-update
  62.2 42.7 %reduce-scatter.3.cloned.1.call-done = f32[32,16,256]{2,1,0:T(8,128)} async-done(((f32[128,16,256]{2,1,0:T(8,128)}), f32[32,16,256]{2,1,0:T(8,128)}) %reduce-scatter.3.cloned.1.call-update) | async-done | bytes 524304 | tf_op jit(solution)/shard_map/reduce_scatter | solution.py:263
  104.9 1.5 collective-permute-start
  106.4 12.2 %collective-permute-done = f32[16,2,16,256]{3,2,1,0:T(8,128)S(1)} collective-permute-done((f32[16,2,16,256]{3,2,1,0:T(8,128)}, f32[16,2,16,256]{3,2,1,0:T(8,128)S(1)}, u32[]{:S(2)}, u32[]{:S(2)}) %collective-permute-start) | collective-permute-done | bytes 524320 | tf_op jit(solution)/shard_map/ppermute | solution.py:219
  118.6 1.2 pad_maximum_fusion.5
  119.8 1.5 collective-permute-start.1
  121.4 22.5 %collective-permute-done.1 = f32[32,2,16,256]{3,2,1,0:T(8,128)S(1)} collective-permute-done((f32[32,2,16,256]{3,2,1,0:T(8,128)S(1)}, f32[32,2,16,256]{3,2,1,0:T(8,128)S(1)}, u32[]{:S(2)}, u32[]{:S(2)}) %collective-permute-start.1) | collective-permute-done | bytes 1048608 | tf_op jit(solution)/shard_map/ppermute | solution.py:219
  143.8 0.2 pad_maximum_fusion.3
  144.1 4.1 %collective-permute-done.2 = f32[64,2,16,256]{3,2,1,0:T(8,128)S(1)} collective-permute-done((f32[64,2,16,256]{3,2,1,0:T(8,128)S(1)}, f32[64,2,16,256]{3,2,1,0:T(8,128)S(1)}, u32[]{:S(2)}, u32[]{:S(2)}) %collective-permute-start.2) | collective-permute-done | bytes 2097184 | tf_op jit(solution)/shard_map/ppermute | solution.py:219
  148.3 2.4 pad_maximum_fusion.q_ref
  150.7 1.5 collective-permute-start.3
  152.2 12.7 %collective-permute-done.3 = f32[16,2,16,256]{3,2,1,0:T(8,128)S(1)} collective-permute-done((f32[16,2,16,256]{3,2,1,0:T(8,128)}, f32[16,2,16,256]{3,2,1,0:T(8,128)S(1)}, u32[]{:S(2)}, u32[]{:S(2)}) %collective-permute-start.3) | collective-permute-done | bytes 524320 | tf_op jit(solution)/shard_map/ppermute | solution.py:219
  164.9 2.2 pad_maximum_fusion.6
  167.1 1.5 collective-permute-start.4
  168.6 15.7 %shard_map.105 = (f32[16,128,128]{2,1,0:T(8,128)}, f32[16,2,16,256]{3,2,1,0:T(8,128)}) custom-call(s32[16,28]{1,0:T(8,128)S(1)} %fusion.1.far, s32[16,28]{1,0:T(8,128)S(1)} %copy-done.2, f32[128,2,16,256]{3,2,1,0:T(8,128)} %pad_maximum_fusion.q_ref, f32[316,128,128]{2,1,0:T(8,128)} %bitcast.58, f32[16,128,128]{2,1,0:T(8,128)S(1)} %bitcast.53), custom_call_target="tpu_custom_call" | custom-call | tf_op jit(solution)/shard_map/pallas_call | solution.py:135
  184.4 7.3 %collective-permute-done.4 = f32[32,2,16,256]{3,2,1,0:T(8,128)S(1)} collective-permute-done((f32[32,2,16,256]{3,2,1,0:T(8,128)}, f32[32,2,16,256]{3,2,1,0:T(8,128)S(1)}, u32[]{:S(2)}, u32[]{:S(2)}) %collective-permute-start.4) | collective-permute-done | bytes 1048608 | tf_op jit(solution)/shard_map/ppermute | solution.py:219
  191.7 0.2 pad_maximum_fusion.4
  192.0 4.1 %collective-permute-done.5 = f32[64,2,16,256]{3,2,1,0:T(8,128)S(1)} collective-permute-done((f32[64,2,16,256]{3,2,1,0:T(8,128)S(1)}, f32[64,2,16,256]{3,2,1,0:T(8,128)S(1)}, u32[]{:S(2)}, u32[]{:S(2)}) %collective-permute-start.5) | collective-permute-done | bytes 2097184 | tf_op jit(solution)/shard_map/ppermute | solution.py:219
  196.1 2.5 pad_maximum_fusion.1.q_ref
  198.6 15.7 %shard_map.106 = (f32[16,128,128]{2,1,0:T(8,128)}, f32[16,2,16,256]{3,2,1,0:T(8,128)}) custom-call(s32[16,28]{1,0:T(8,128)S(1)} %fusion.1.far, s32[16,28]{1,0:T(8,128)S(1)} %copy-done.2, f32[128,2,16,256]{3,2,1,0:T(8,128)} %pad_maximum_fusion.1.q_ref, f32[316,128,128]{2,1,0:T(8,128)} %bitcast.59, ...), custom_call_target="tpu_custom_call", output_to_operand_aliasing={{0}: (5, {})} | custom-call | tf_op jit(solution)/shard_map/pallas_call | solution.py:135
  214.3 0.1 copy.44
  214.4 15.2 %all-gather.8.cloned.1.call-done = f32[64,2,16,256]{3,2,1,0:T(8,128)} async-done(((f32[16,2,16,256]{3,2,1,0:T(8,128)}), f32[64,2,16,256]{3,2,1,0:T(8,128)}) %all-gather.8.cloned.1.call-update) | async-done | bytes 2097168 | tf_op jit(solution)/shard_map/all_gather | solution.py:279
  229.6 46.5 %all-gather.10.cloned.1.call-done = f32[64,2,16,256]{3,2,1,0:T(8,128)} async-done(((f32[16,2,16,256]{3,2,1,0:T(8,128)}), f32[64,2,16,256]{3,2,1,0:T(8,128)}) %all-gather.10.cloned.1.call-update) | async-done | bytes 2097168 | tf_op jit(solution)/shard_map/all_gather | solution.py:279
  276.0 10.3 %shard_map.107 = f32[32,128,128]{2,1,0:T(8,128)} custom-call(s32[32]{0:T(128)S(1)} %get-tuple-element.23.parent, s32[32]{0:T(128)S(1)} %get-tuple-element.22.octant, f32[4,16,2,16,256]{4,3,2,1,0:T(8,128)} %bitcast.68, f32[4,16,2,16,256]{4,3,2,1,0:T(8,128)} %bitcast.69, f32[128,256]{1,0:T(8,128)S(1)} %bitcast.56, f32[256,128]{1,0:T(8,128)S(1)} %bitcast.57, ...), custom_call_target="tpu_custom_call" | custom-call | tf_op jit(solution)/shard_map/pallas_call | solution.py:193
  (32 shorter events, 0.7 us)
Async XLA Ops:
  7.2 33.6 %all-gather.6.cloned.1.call-start = ((), (), s32[]{:S(2)}) async-start(), calls=%async_computation.2 | async-start | bytes 1310720 | tf_op jit(solution)/shard_map/all_gather | solution.py:257
  9.0 96.0 %reduce-scatter.3.cloned.1.call-start = ((), (), s32[]{:S(2)}) async-start(), calls=%async_computation.3 | async-start | bytes 2621440 | tf_op jit(solution)/shard_map/reduce_scatter | solution.py:263
  45.5 1.5 copy-start.1
  61.4 89.3 %reduce-scatter.5.cloned.1.call-start = ((), (), s32[]{:S(2)}) async-start(), calls=%async_computation.4 | async-start | bytes 2621440 | tf_op jit(solution)/shard_map/reduce_scatter | solution.py:263
  62.2 167.4 %all-gather.8.cloned.1.call-start = ((), (), s32[]{:S(2)}) async-start(), calls=%async_computation.5 | async-start | bytes 2621440 | tf_op jit(solution)/shard_map/all_gather | solution.py:279
  104.9 38.9 %copy-start.4 = (f32[32,16,256]{2,1,0:T(8,128)S(1)}, f32[32,16,256]{2,1,0:T(8,128)}, u32[]{:S(2)}) copy-start(f32[32,16,256]{2,1,0:T(8,128)} %reduce-scatter.3.cloned.1.call-done) | copy-start | bytes 1572868
  104.9 13.7 %collective-permute-start = (f32[16,2,16,256]{3,2,1,0:T(8,128)}, f32[16,2,16,256]{3,2,1,0:T(8,128)S(1)}, u32[]{:S(2)}, u32[]{:S(2)}) collective-permute-start(f32[16,2,16,256]{3,2,1,0:T(8,128)} %bitcast.64), channel_id=1, source_target_pairs={{0,16},{4,20},{8,24},{12,28},{16,0},{20,4},{24,8},{28,12},{1,17},{... | collective-permute-start | bytes 1572872 | tf_op jit(solution)/shard_map/ppermute | solution.py:219
  119.8 24.0 %collective-permute-start.1 = (f32[32,2,16,256]{3,2,1,0:T(8,128)S(1)}, f32[32,2,16,256]{3,2,1,0:T(8,128)S(1)}, u32[]{:S(2)}, u32[]{:S(2)}) collective-permute-start(f32[32,2,16,256]{3,2,1,0:T(8,128)S(1)} %pad_maximum_fusion.5), channel_id=1, source_target_pairs={{0,8},{4,12},{8,0},{12,4},{16,24},{20,28},{24,16},{28,20},{1,9},{5... | collective-permute-start | bytes 3145736 | tf_op jit(solution)/shard_map/ppermute | solution.py:219
  144.0 4.2 %collective-permute-start.2 = (f32[64,2,16,256]{3,2,1,0:T(8,128)S(1)}, f32[64,2,16,256]{3,2,1,0:T(8,128)S(1)}, u32[]{:S(2)}, u32[]{:S(2)}) collective-permute-start(f32[64,2,16,256]{3,2,1,0:T(8,128)S(1)} %pad_maximum_fusion.3), channel_id=1, source_target_pairs={{0,4},{4,0},{8,12},{12,8},{16,20},{20,16},{24,28},{28,24},{1,5},{5... | collective-permute-start | bytes 6291464 | tf_op jit(solution)/shard_map/ppermute | solution.py:219
  150.7 17.9 %copy-start.5 = (s32[16,28]{1,0:T(8,128)S(1)}, s32[16,28]{1,0:T(8,128)}, u32[]{:S(2)}) copy-start(s32[16,28]{1,0:T(8,128)} %param.16) | copy-start | bytes 5380
  150.7 17.9 %copy-start = (f32[16,2,8192]{2,1,0:T(2,128)S(1)}, f32[16,2,8192]{2,1,0:T(2,128)}, u32[]{:S(2)}) copy-start(f32[16,2,8192]{2,1,0:T(2,128)} %param.14) | copy-start | bytes 3145732
  150.7 17.9 %copy-start.2 = (s32[16,28]{1,0:T(8,128)S(1)}, s32[16,28]{1,0:T(8,128)}, u32[]{:S(2)}) copy-start(s32[16,28]{1,0:T(8,128)} %kind.3) | copy-start | bytes 5380
  150.7 14.2 %collective-permute-start.3 = (f32[16,2,16,256]{3,2,1,0:T(8,128)}, f32[16,2,16,256]{3,2,1,0:T(8,128)S(1)}, u32[]{:S(2)}, u32[]{:S(2)}) collective-permute-start(f32[16,2,16,256]{3,2,1,0:T(8,128)} %bitcast.60), channel_id=1, source_target_pairs={{0,16},{4,20},{8,24},{12,28},{16,0},{20,4},{24,8},{28,12},{1,17},{... | collective-permute-start | bytes 1572872 | tf_op jit(solution)/shard_map/ppermute | solution.py:219
  167.1 24.6 %collective-permute-start.4 = (f32[32,2,16,256]{3,2,1,0:T(8,128)}, f32[32,2,16,256]{3,2,1,0:T(8,128)S(1)}, u32[]{:S(2)}, u32[]{:S(2)}) collective-permute-start(f32[32,2,16,256]{3,2,1,0:T(8,128)} %pad_maximum_fusion.6), channel_id=1, source_target_pairs={{0,8},{4,12},{8,0},{12,4},{16,24},{20,28},{24,16},{28,20},{1,9},{5... | collective-permute-start | bytes 3145736 | tf_op jit(solution)/shard_map/ppermute | solution.py:219
  168.6 23.1 %copy-start.3 = (f32[32,16,256]{2,1,0:T(8,128)S(1)}, f32[32,16,256]{2,1,0:T(8,128)}, u32[]{:S(2)}) copy-start(f32[32,16,256]{2,1,0:T(8,128)} %reduce-scatter.5.cloned.1.call-done) | copy-start | bytes 1572868
  184.4 91.7 %all-gather.10.cloned.1.call-start = ((), (), s32[]{:S(2)}) async-start(), calls=%async_computation.6 | async-start | bytes 2621440 | tf_op jit(solution)/shard_map/all_gather | solution.py:279
  191.9 4.2 %collective-permute-start.5 = (f32[64,2,16,256]{3,2,1,0:T(8,128)S(1)}, f32[64,2,16,256]{3,2,1,0:T(8,128)S(1)}, u32[]{:S(2)}, u32[]{:S(2)}) collective-permute-start(f32[64,2,16,256]{3,2,1,0:T(8,128)S(1)} %pad_maximum_fusion.4), channel_id=1, source_target_pairs={{0,4},{4,0},{8,12},{12,8},{16,20},{20,16},{24,28},{28,24},{1,5},{5... | collective-permute-start | bytes 6291464 | tf_op jit(solution)/shard_map/ppermute | solution.py:219
Sparse Core Ops, SparseCore 0:
  10.1 30.6 all-gather.5
  61.5 43.3 reduce-scatter.2
  107.3 43.1 reduce-scatter.4
  184.5 45.0 all-gather.7
  231.6 44.4 all-gather.9
